TPU v7x, 128 devices: a whole 4x4x4 slice. The times are simulated.
128 devices in a mesh: row: 8 (over y, core), col: 16 (over z, x).
Axes of the slice: x: 4, y: 4, z: 4, core: 2. Of those that a mesh axis runs over, the one named last changes fastest.
Arguments:
- inputs: bfloat16 [1280, 6144], P('col', 'row'), may hold values from -6 to 6
- w_in: bfloat16 [6144, 24576], P('row', 'col'), may hold values from -0.078125 to 0.078125
- b_in: float32 [24576], P('col'), may hold values from -3 to 3
- w_out: bfloat16 [24576, 6144], P('col', 'row'), may hold values from -0.0390625 to 0.0390625
- b_out: float32 [6144], P('row'), may hold values from -3 to 3
- out_grad: bfloat16 [1280, 6144], P('col', 'row'), may hold values from -0.625 to 0.625
Outputs:
- output: bfloat16 [1280, 6144], P('col', 'row')
- input_grad: bfloat16 [1280, 6144], P('col', 'row')
- w_in_grad: float32 [6144, 24576], P('row', 'col')
- b_in_grad: float32 [24576], P('col')
- w_out_grad: float32 [24576, 6144], P('col', 'row')
- b_out_grad: float32 [6144], P('row')
All inputs are finite; a program needn't handle non-finite values.
Results may differ from a plain program's by a relative error of at most 0.007.
Values may be sent and summed in bfloat16 or wider, within the bound.
A program may use at most 128 MiB of HBM per device.

v0:
```python
import jax
import jax.numpy as jnp
from jax import lax
from jax.sharding import PartitionSpec as P


def gelu_parts(hidden):
    half = 0.5 * (1.0 + jax.scipy.special.erf(hidden * 0.7071067811865476))
    slope = half + hidden * jnp.exp(-0.5 * hidden * hidden) * 0.3989422804014327
    return (hidden * half, slope)


def shards(inputs, w_in, b_in, w_out, b_out, out_grad):
    inputs_all, grad_all = (
        lax.all_gather(inputs, "col", axis=0, tiled=True),
        lax.all_gather(out_grad, "col", axis=0, tiled=True),
    )
    partial_value = jnp.dot(inputs_all, w_in, preferred_element_type=jnp.float32)
    hidden = lax.psum(partial_value, "row") + b_in
    act, slope = gelu_parts(hidden)
    act_all = act.astype(jnp.bfloat16)
    rows = act_all
    output = (
        lax.psum_scatter(
            jnp.dot(rows, w_out, preferred_element_type=jnp.float32),
            "col",
            scatter_dimension=0,
            tiled=True,
        )
        + b_out
    ).astype(jnp.bfloat16)
    b_out_grad = jnp.sum(grad_all, axis=0, dtype=jnp.float32)
    w_out_grad = jnp.einsum("tf,td->fd", act_all, grad_all, preferred_element_type=jnp.float32)
    partial_grad = jnp.einsum("td,fd->tf", grad_all, w_out, preferred_element_type=jnp.float32)
    act_grad = lax.psum(partial_grad, "row")
    pre_grad = (act_grad * slope).astype(jnp.bfloat16)
    b_in_grad = jnp.sum(pre_grad, axis=0, dtype=jnp.float32)
    w_in_grad = jnp.einsum("td,tf->df", inputs_all, pre_grad, preferred_element_type=jnp.float32)
    rows = pre_grad
    input_grad = lax.psum_scatter(
        jnp.einsum("tf,df->td", rows, w_in, preferred_element_type=jnp.float32),
        "col",
        scatter_dimension=0,
        tiled=True,
    ).astype(jnp.bfloat16)
    return (output, input_grad, w_in_grad, b_in_grad, w_out_grad, b_out_grad)


def solution(mesh):
    placed = (
        P("col", "row"),
        P("row", "col"),
        P("col"),
        P("col", "row"),
        P("row"),
        P("col", "row"),
    )
    return jax.shard_map(
        shards,
        mesh=mesh,
        in_specs=placed,
        out_specs=(
            P("col", "row"),
            P("col", "row"),
            P("row", "col"),
            P("col"),
            P("col", "row"),
            P("row"),
        ),
        check_vma=False,
    )
```

profile of v0, /device:TPU:0, one launch (start us, length us, event | category | flops | bytes accessed | tf_op | source)
XLA Modules:
  0.0 465.8 jit_solution(393771307948937727)
XLA Ops:
  7.2 0.0 copy-start
  7.2 0.0 all-gather.5.cloned.1.call-start
  7.2 0.7 all-gather.5.cloned.1.call-update
  7.9 0.0 all-gather.3.cloned.1.call-start
  8.0 0.7 all-gather.3.cloned.1.call-update
  8.7 0.0 all-reduce.3.cloned.1.call-start
  8.7 48.7 %all-gather.5.cloned.1.call-done = bf16[1280,768]{1,0:T(8,128)(2,1)} async-done(((bf16[80,768]{1,0:T(8,128)(2,1)}), bf16[1280,768]{1,0:T(8,128)(2,1)}) %all-gather.5.cloned.1.call-update) | async-done | bytes 1966096 | tf_op jit(solution)/shard_map/all_gather | solution.py:16
  57.4 8.7 %fusion.9 = f32[1280,1536]{1,0:T(8,128)} fusion(bf16[1280,768]{1,0:T(8,128)(2,1)} %all-gather.5.cloned.1.call-done, bf16[1536,768]{1,0:T(8,128)(2,1)} %param.9), kind=kOutput, calls=%fused_computation.15 | convolution fusion | flops 3019898880 | bytes 12189696 | tf_op jit(solution)/shard_map/td,fd->tf/dot_general | solution.py:34
  66.1 37.5 %all-gather.3.cloned.1.call-done = bf16[1280,768]{1,0:T(8,128)(2,1)} async-done(((bf16[80,768]{1,0:T(8,128)(2,1)}), bf16[1280,768]{1,0:T(8,128)(2,1)}) %all-gather.3.cloned.1.call-update) | async-done | bytes 1966096 | tf_op jit(solution)/shard_map/all_gather | solution.py:15
  103.5 7.0 %fusion.7 = f32[1280,1536]{1,0:T(8,128)} fusion(bf16[1280,768]{1,0:T(8,128)(2,1)} %all-gather.3.cloned.1.call-done, bf16[768,1536]{1,0:T(8,128)(2,1)S(1)} %copy-done), kind=kOutput, calls=%fused_computation.13 | convolution fusion | flops 3019898880 | bytes 12189696 | tf_op jit(solution)/shard_map/dot_general | solution.py:18
  110.5 0.0 all-reduce.3.cloned.1.call-update
  110.5 0.0 reduce-scatter.5.cloned.1.call-start
  110.6 173.0 %all-reduce.3.cloned.1.call-done = (f32[1280,1536]{1,0:T(8,128)}, f32[1280,1536]{1,0:T(8,128)}) async-done(((f32[1280,1536]{1,0:T(8,128)}, f32[1280,1536]{1,0:T(8,128)}), (f32[1280,1536]{1,0:T(8,128)}, f32[1280,1536]{1,0:T(8,128)})) %all-reduce.3.cloned.1.call-update) | async-done | bytes 15728656 | tf_op jit(solution)/shard_map/psum | solution.py:19
  283.6 0.0 copy-done.4
  283.6 10.6 %convert_reduce_fusion = (f32[1536]{0:T(1024)}, bf16[1280,1536]{1,0:T(8,128)(2,1)S(1)}, bf16[1280,1536]{1,0:T(8,128)(2,1)}) fusion(f32[1280,1536]{1,0:T(8,128)} %get-tuple-element.13, f32[1280,1536]{1,0:T(8,128)} %get-tuple-element.12, f32[1536]{0:T(1024)S(1)} %copy-done.4), kind=kLoop, calls=%fused_computation.7 | loop fusion | flops 29489664 | bytes 23605248 | tf_op jit(solution)/shard_map/reduce_sum | solution.py:37
  294.2 1.9 copy-done.2
  296.1 5.1 %fusion.10 = f32[1280,768]{1,0:T(8,128)} fusion(bf16[1280,1536]{1,0:T(8,128)(2,1)S(1)} %get-tuple-element.15, bf16[768,1536]{1,0:T(8,128)(2,1)S(1)} %copy-done), kind=kOutput, calls=%fused_computation.16 | convolution fusion | flops 3019898880 | bytes 10223616 | tf_op jit(solution)/shard_map/tf,df->td/dot_general | solution.py:41
  301.2 0.0 reduce-scatter.5.cloned.1.call-update
  301.3 0.2 reduce-scatter.3.cloned.1.call-start
  301.5 1.4 copy-done.6
  302.9 7.2 %fusion.8 = f32[1280,768]{1,0:T(8,128)} fusion(bf16[1280,1536]{1,0:T(8,128)(2,1)} %get-tuple-element.16, bf16[1536,768]{1,0:T(8,128)(2,1)S(1)} %copy-done.6), kind=kOutput, calls=%fused_computation.14 | convolution fusion | flops 3019898880 | bytes 10223616 | tf_op jit(solution)/shard_map/dot_general | solution.py:25
  310.1 0.0 reduce-scatter.3.cloned.1.call-update
  310.1 1.6 copy-done.3
  311.7 0.9 convert_reduce_fusion.1
  312.6 8.2 %convolution_bitcast_fusion = f32[768,1536]{0,1:T(8,128)} fusion(bf16[1280,1536]{1,0:T(8,128)(2,1)} %copy-done.2, bf16[1280,768]{1,0:T(8,128)(2,1)} %all-gather.3.cloned.1.call-done), kind=kOutput, calls=%fused_computation.11 | convolution fusion | flops 3019898880 | bytes 10616832 | tf_op jit(solution)/shard_map/td,tf->df/dot_general | solution.py:38
  320.8 6.1 %copy.12 = f32[768,1536]{1,0:T(8,128)} copy(f32[768,1536]{0,1:T(8,128)} %convolution_bitcast_fusion) | data formatting | bytes 9437184
  327.0 8.4 %fusion.11 = f32[1536,768]{1,0:T(8,128)} fusion(bf16[1280,1536]{1,0:T(8,128)(2,1)} %get-tuple-element.16, bf16[1280,768]{1,0:T(8,128)(2,1)} %all-gather.5.cloned.1.call-done), kind=kOutput, calls=%fused_computation.17 | convolution fusion | flops 3019898880 | bytes 10616832 | tf_op jit(solution)/shard_map/tf,td->fd/dot_general | solution.py:33
  335.4 42.9 %reduce-scatter.5.cloned.1.call-done = f32[80,768]{1,0:T(8,128)} async-done(((f32[1280,768]{1,0:T(8,128)}), f32[80,768]{1,0:T(8,128)}) %reduce-scatter.5.cloned.1.call-update) | async-done | bytes 245776 | tf_op jit(solution)/shard_map/reduce_scatter | solution.py:40
  378.3 1.6 convert_element_type.21
  379.9 77.8 %reduce-scatter.3.cloned.1.call-done = f32[80,768]{1,0:T(8,128)} async-done(((f32[1280,768]{1,0:T(8,128)}), f32[80,768]{1,0:T(8,128)}) %reduce-scatter.3.cloned.1.call-update) | async-done | bytes 245776 | tf_op jit(solution)/shard_map/reduce_scatter | solution.py:24
  457.7 0.0 copy-done.5
  457.7 1.6 add_convert_fusion
  (8 shorter events, 0.0 us)
Async XLA Ops:
  7.2 96.4 %copy-start = (bf16[768,1536]{1,0:T(8,128)(2,1)S(1)}, bf16[768,1536]{1,0:T(8,128)(2,1)}, u32[]{:S(2)}) copy-start(bf16[768,1536]{1,0:T(8,128)(2,1)} %param.7) | copy-start | bytes 7077892
  7.2 50.2 %all-gather.5.cloned.1.call-start = ((), (), s32[]{:S(2)}) async-start(), calls=%async_computation.4 | async-start | bytes 2088960 | tf_op jit(solution)/shard_map/all_gather | solution.py:16
  7.9 95.6 %all-gather.3.cloned.1.call-start = ((), (), s32[]{:S(2)}) async-start(), calls=%async_computation.2 | async-start | bytes 2088960 | tf_op jit(solution)/shard_map/all_gather | solution.py:15
  8.7 274.9 %all-reduce.3.cloned.1.call-start = ((), (), s32[]{:S(2)}) async-start(), calls=%async_computation.6 | async-start | bytes 31457280 | tf_op jit(solution)/shard_map/psum | solution.py:19
  110.5 173.1 %copy-start.4 = (f32[1536]{0:T(1024)S(1)}, f32[1536]{0:T(1024)}, u32[]{:S(2)}) copy-start(f32[1536]{0:T(1024)} %param.8) | copy-start | bytes 18436
  110.5 267.7 %reduce-scatter.5.cloned.1.call-start = ((), (), s32[]{:S(2)}) async-start(), calls=%async_computation.5 | async-start | bytes 4177920 | tf_op jit(solution)/shard_map/reduce_scatter | solution.py:40
  294.2 1.9 copy-start.2
  301.2 1.7 copy-start.6
  301.3 156.4 %reduce-scatter.3.cloned.1.call-start = ((), (), s32[]{:S(2)}) async-start(), calls=%async_computation.3 | async-start | bytes 4177920 | tf_op jit(solution)/shard_map/reduce_scatter | solution.py:24
  310.1 1.6 copy-start.3
  327.0 130.7 %copy-start.5 = (f32[768]{0:T(1024)S(1)}, f32[768]{0:T(1024)}, u32[]{:S(2)}) copy-start(f32[768]{0:T(1024)} %param.10) | copy-start | bytes 9220
  327.0 132.3 %copy-start.1 = (bf16[768,1536]{1,0:T(8,128)(2,1)S(1)}, bf16[768,1536]{1,0:T(8,128)(2,1)}, u32[]{:S(2)}) copy-start(bf16[768,1536]{1,0:T(8,128)(2,1)} %param.7) | copy-start | bytes 7077892
Sparse Core Ops, SparseCore 0:
  10.2 47.1 all-gather.4
  59.5 43.9 all-gather.2
  110.6 172.8 all-reduce.2
  301.4 76.8 reduce-scatter.4
  381.5 76.1 reduce-scatter.2
where the time goes:
time: 466 us
  waiting for transfers between devices  381 us (82%)
  matrix products  44.6 us (10%)
  other arithmetic  14.7 us (3%)
  between operations  13.8 us (3%)
  local copies, waits for them, and re-layouts  11 us (2%)
    psum x1, waiting for transfers between devices, shards(): hidden = lax.psum(partial_value, 'row') + b_in  173 us
    reduce_scatter x1, waiting for transfers between devices, shards(): lax.psum_scatter(jnp.dot(rows, w_out, preferred_element_type=jnp.float32)...  77.8 us
    all_gather x1, waiting for transfers between devices, shards(): lax.all_gather(out_grad, 'col', axis=0, tiled=True)  48.7 us
    reduce_scatter x1, waiting for transfers between devices, shards(): lax.psum_scatter(jnp.einsum('tf,df->td', rows, w_in, preferred_element_ty...  42.9 us
    all_gather x1, waiting for transfers between devices, shards(): lax.all_gather(inputs, 'col', axis=0, tiled=True)  37.5 us
    unnamed x15, local copies, waits for them, and re-layouts  11 us
    reduce_sum x1, other arithmetic, shards(): b_in_grad = jnp.sum(pre_grad, axis=0, dtype=jnp.float32)  10.6 us
  transfers between devices with their start and end apart: 5, of which 5 were waited for; matrix products, arithmetic and copies ran while one was open for 9% of the time, Pallas kernels for 0%

commit v1 on v0

--- a/solution.py
+++ b/solution.py
@@ -16,7 +16,7 @@
         lax.all_gather(out_grad, "col", axis=0, tiled=True),
     )
     partial_value = jnp.dot(inputs_all, w_in, preferred_element_type=jnp.float32)
-    hidden = lax.psum(partial_value, "row") + b_in
+    hidden = jnp.sum(lax.all_gather(partial_value, "row"), axis=0) + b_in
     act, slope = gelu_parts(hidden)
     act_all = act.astype(jnp.bfloat16)
     rows = act_all

time: 466 us -> 668 us (1.43)
  waiting for transfers between devices: 381 us -> 558 us
  other arithmetic: 14.7 us -> 39.4 us
    all_gather x0 -> x1, waiting for transfers between devices: none -> 271 us  [shards(): hidden = jnp.sum(lax.all_gather(partial_value, 'row'), axis=0) + b_in]
    psum x1, waiting for transfers between devices: 173 us -> 77.1 us  [shards(): act_grad = lax.psum(partial_grad, 'row')]
    reduce_sum x0 -> x1, other arithmetic: none -> 24.7 us  [shards(): hidden = jnp.sum(lax.all_gather(partial_value, 'row'), axis=0) + b_in]
    all_gather x1, waiting for transfers between devices: 37.5 us -> 48.7 us  [shards(): lax.all_gather(inputs, 'col', axis=0, tiled=True)]
    all_gather x1, waiting for transfers between devices: 48.7 us -> 39.1 us  [shards(): lax.all_gather(out_grad, 'col', axis=0, tiled=True)]
  transfers between devices with their start and end apart: 5 -> 6, of which waited for: 5 -> 6; matrix products, arithmetic and copies ran while one was open for 9% -> 11% of each run, Pallas kernels for 0% -> 0%
where the time goes in v1:
time: 668 us
  waiting for transfers between devices  558 us (84%)
  matrix products  44.5 us (7%)
  other arithmetic  39.4 us (6%)
  between operations  14.1 us (2%)
  local copies, waits for them, and re-layouts  11 us (2%)
    all_gather x1, waiting for transfers between devices, shards(): hidden = jnp.sum(lax.all_gather(partial_value, 'row'), axis=0) + b_in  271 us
    reduce_scatter x1, waiting for transfers between devices, shards(): lax.psum_scatter(jnp.dot(rows, w_out, preferred_element_type=jnp.float32)...  77.9 us
    psum x1, waiting for transfers between devices, shards(): act_grad = lax.psum(partial_grad, 'row')  77.1 us
    all_gather x1, waiting for transfers between devices, shards(): lax.all_gather(inputs, 'col', axis=0, tiled=True)  48.7 us
    reduce_scatter x1, waiting for transfers between devices, shards(): lax.psum_scatter(jnp.einsum('tf,df->td', rows, w_in, preferred_element_ty...  42.8 us
    all_gather x1, waiting for transfers between devices, shards(): lax.all_gather(out_grad, 'col', axis=0, tiled=True)  39.1 us
    reduce_sum x1, other arithmetic, shards(): hidden = jnp.sum(lax.all_gather(partial_value, 'row'), axis=0) + b_in  24.7 us
  transfers between devices with their start and end apart: 6, of which 6 were waited for; matrix products, arithmetic and copies ran while one was open for 11% of the time, Pallas kernels for 0%

profile of v1, /device:TPU:0, one launch (start us, length us, event | category | flops | bytes accessed | tf_op | source)
XLA Modules:
  0.0 668.0 jit_solution(8866211675892188899)
XLA Ops:
  7.2 0.0 all-gather.5.cloned.1.call-start
  7.2 0.7 all-gather.5.cloned.1.call-update
  7.9 0.0 all-gather.7.cloned.1.call-start
  8.0 0.7 all-gather.7.cloned.1.call-update
  8.7 0.0 all-gather.9.cloned.1.call-start
  8.7 48.7 %all-gather.5.cloned.1.call-done = bf16[1280,768]{1,0:T(8,128)(2,1)} async-done(((bf16[80,768]{1,0:T(8,128)(2,1)}), bf16[1280,768]{1,0:T(8,128)(2,1)}) %all-gather.5.cloned.1.call-update) | async-done | bytes 1966096 | tf_op jit(solution)/shard_map/all_gather | solution.py:15
  57.4 7.0 %fusion.7 = f32[1280,1536]{1,0:T(8,128)} fusion(bf16[1280,768]{1,0:T(8,128)(2,1)} %all-gather.5.cloned.1.call-done, bf16[768,1536]{1,0:T(8,128)(2,1)S(1)} %copy-done), kind=kOutput, calls=%fused_computation.13 | convolution fusion | flops 3019898880 | bytes 12189696 | tf_op jit(solution)/shard_map/dot_general | solution.py:18
  64.3 0.0 all-gather.9.cloned.1.call-update
  64.4 0.0 all-reduce.2.cloned.1.call-start
  64.4 39.1 %all-gather.7.cloned.1.call-done = bf16[1280,768]{1,0:T(8,128)(2,1)} async-done(((bf16[80,768]{1,0:T(8,128)(2,1)}), bf16[1280,768]{1,0:T(8,128)(2,1)}) %all-gather.7.cloned.1.call-update) | async-done | bytes 1966096 | tf_op jit(solution)/shard_map/all_gather | solution.py:16
  103.5 8.6 %fusion.9 = f32[1280,1536]{1,0:T(8,128)} fusion(bf16[1280,768]{1,0:T(8,128)(2,1)} %all-gather.7.cloned.1.call-done, bf16[1536,768]{1,0:T(8,128)(2,1)} %param.9), kind=kOutput, calls=%fused_computation.15 | convolution fusion | flops 3019898880 | bytes 12189696 | tf_op jit(solution)/shard_map/td,fd->tf/dot_general | solution.py:34
  112.1 0.0 all-reduce.2.cloned.1.call-update
  112.2 0.0 reduce-scatter.5.cloned.1.call-start
  112.2 271.4 %all-gather.9.cloned.1.call-done = f32[10240,1536]{1,0:T(8,128)} async-done(((f32[1280,1536]{1,0:T(8,128)}), f32[10240,1536]{1,0:T(8,128)}) %all-gather.9.cloned.1.call-update) | async-done | bytes 62914576 | tf_op jit(solution)/shard_map/all_gather | solution.py:19
  383.6 24.7 %reduce_sum.27 = f32[1280,1536]{1,0:T(8,128)} reduce(f32[8,1280,1536]{2,1,0:T(8,128)} %bitcast.15, f32[]{:T(128)} %constant.0.clone.1), dimensions={0}, to_apply=%region_0.0 | reduce | flops 13762560 | bytes 70778880 | tf_op jit(solution)/shard_map/reduce_sum | solution.py:19
  408.3 77.1 %all-reduce.2.cloned.1.call-done = f32[1280,1536]{1,0:T(8,128)} async-done(((f32[1280,1536]{1,0:T(8,128)}), f32[1280,1536]{1,0:T(8,128)}) %all-reduce.2.cloned.1.call-update) | async-done | bytes 7864336 | tf_op jit(solution)/shard_map/psum | solution.py:35
  485.4 10.6 %convert_reduce_fusion = (f32[1536]{0:T(1024)}, bf16[1280,1536]{1,0:T(8,128)(2,1)S(1)}, bf16[1280,1536]{1,0:T(8,128)(2,1)}) fusion(f32[1280,1536]{1,0:T(8,128)} %all-reduce.2.cloned.1.call-done, f32[1280,1536]{1,0:T(8,128)} %reduce_sum.27, f32[1536]{0:T(1024)S(1)} %copy-done.4), kind=kLoop, calls=%fused_computation.7 | loop fusion | flops 29489664 | bytes 23605248 | tf_op jit(solution)/shard_map/reduce_sum | solution.py:37
  496.0 1.9 copy-done.2
  497.9 5.1 fusion.10
  503.0 0.0 reduce-scatter.5.cloned.1.call-update
  503.1 0.2 reduce-scatter.3.cloned.1.call-start
  503.3 1.4 copy-done.6
  504.7 7.2 %fusion.8 = f32[1280,768]{1,0:T(8,128)} fusion(bf16[1280,1536]{1,0:T(8,128)(2,1)} %get-tuple-element.14, bf16[1536,768]{1,0:T(8,128)(2,1)S(1)} %copy-done.6), kind=kOutput, calls=%fused_computation.14 | convolution fusion | flops 3019898880 | bytes 10223616 | tf_op jit(solution)/shard_map/dot_general | solution.py:25
  511.9 1.6 copy-done.3
  513.5 0.9 convert_reduce_fusion.1
  514.4 8.2 %convolution_bitcast_fusion = f32[768,1536]{0,1:T(8,128)} fusion(bf16[1280,1536]{1,0:T(8,128)(2,1)} %copy-done.2, bf16[1280,768]{1,0:T(8,128)(2,1)} %all-gather.5.cloned.1.call-done), kind=kOutput, calls=%fused_computation.11 | convolution fusion | flops 3019898880 | bytes 10616832 | tf_op jit(solution)/shard_map/td,tf->df/dot_general | solution.py:38
  522.6 6.1 copy.12
  528.7 8.4 %fusion.11 = f32[1536,768]{1,0:T(8,128)} fusion(bf16[1280,1536]{1,0:T(8,128)(2,1)} %get-tuple-element.14, bf16[1280,768]{1,0:T(8,128)(2,1)} %all-gather.7.cloned.1.call-done), kind=kOutput, calls=%fused_computation.17 | convolution fusion | flops 3019898880 | bytes 10616832 | tf_op jit(solution)/shard_map/tf,td->fd/dot_general | solution.py:33
  537.2 42.8 %reduce-scatter.5.cloned.1.call-done = f32[80,768]{1,0:T(8,128)} async-done(((f32[1280,768]{1,0:T(8,128)}), f32[80,768]{1,0:T(8,128)}) %reduce-scatter.5.cloned.1.call-update) | async-done | bytes 245776 | tf_op jit(solution)/shard_map/reduce_scatter | solution.py:40
  580.0 1.6 convert_element_type.21
  581.6 77.9 %reduce-scatter.3.cloned.1.call-done = f32[80,768]{1,0:T(8,128)} async-done(((f32[1280,768]{1,0:T(8,128)}), f32[80,768]{1,0:T(8,128)}) %reduce-scatter.3.cloned.1.call-update) | async-done | bytes 245776 | tf_op jit(solution)/shard_map/reduce_scatter | solution.py:24
  659.5 1.6 add_convert_fusion
  (12 shorter events, 0.0 us)
Async XLA Ops:
  7.2 50.2 %copy-start = (bf16[768,1536]{1,0:T(8,128)(2,1)S(1)}, bf16[768,1536]{1,0:T(8,128)(2,1)}, u32[]{:S(2)}) copy-start(bf16[768,1536]{1,0:T(8,128)(2,1)} %param.7) | copy-start | bytes 7077892
  7.2 50.2 %all-gather.5.cloned.1.call-start = ((), (), s32[]{:S(2)}) async-start(), calls=%async_computation.2 | async-start | bytes 2088960 | tf_op jit(solution)/shard_map/all_gather | solution.py:15
  7.9 95.6 %all-gather.7.cloned.1.call-start = ((), (), s32[]{:S(2)}) async-start(), calls=%async_computation.4 | async-start | bytes 2088960 | tf_op jit(solution)/shard_map/all_gather | solution.py:16
  8.7 374.9 %all-gather.9.cloned.1.call-start = ((), (), s32[]{:S(2)}) async-start(), calls=%async_computation.7 | async-start | bytes 70778880 | tf_op jit(solution)/shard_map/all_gather | solution.py:19
  64.4 421.0 %all-reduce.2.cloned.1.call-start = ((), (), s32[]{:S(2)}) async-start(), calls=%async_computation.5 | async-start | bytes 15728640 | tf_op jit(solution)/shard_map/psum | solution.py:35
  112.2 467.8 %reduce-scatter.5.cloned.1.call-start = ((), (), s32[]{:S(2)}) async-start(), calls=%async_computation.6 | async-start | bytes 4177920 | tf_op jit(solution)/shard_map/reduce_scatter | solution.py:40
  383.6 101.8 %copy-start.4 = (f32[1536]{0:T(1024)S(1)}, f32[1536]{0:T(1024)}, u32[]{:S(2)}) copy-start(f32[1536]{0:T(1024)} %param.8) | copy-start | bytes 18436
  496.0 1.9 copy-start.2
  503.0 1.7 copy-start.6
  503.1 156.4 %reduce-scatter.3.cloned.1.call-start = ((), (), s32[]{:S(2)}) async-start(), calls=%async_computation.3 | async-start | bytes 4177920 | tf_op jit(solution)/shard_map/reduce_scatter | solution.py:24
  511.9 1.6 copy-start.3
  528.7 130.8 %copy-start.5 = (f32[768]{0:T(1024)S(1)}, f32[768]{0:T(1024)}, u32[]{:S(2)}) copy-start(f32[768]{0:T(1024)} %param.10) | copy-start | bytes 9220
  528.7 132.4 %copy-start.1 = (bf16[768,1536]{1,0:T(8,128)(2,1)S(1)}, bf16[768,1536]{1,0:T(8,128)(2,1)}, u32[]{:S(2)}) copy-start(bf16[768,1536]{1,0:T(8,128)(2,1)} %param.7) | copy-start | bytes 7077892
Sparse Core Ops, SparseCore 0:
  10.2 47.1 all-gather.4
  59.5 43.9 all-gather.6
  105.2 278.3 all-gather.8
  385.8 99.5 all-reduce.1
  503.2 76.7 reduce-scatter.4
  583.2 76.2 reduce-scatter.2
